TPU v7x, 32 devices: a whole 2x2x4 slice. The times are simulated.
32 devices in a mesh: row: 8 (over y, x, core), col: 4 (over z).
Axes of the slice: x: 2, y: 2, z: 4, core: 2. Of those that a mesh axis runs over, the one named last changes fastest.
Arguments:
- coeffs: bfloat16 [16384, 1024], P('row', 'col'), may hold values from -6 to 6
- intersection: bfloat16 [16384, 16384], P('row', 'col'), may hold values from -0.006225586 to 0.006225586
- coeff_mask: int32 [128, 8], P('row', 'col'), may hold values 0 or 1
- intersection_mask: int32 [128, 128], P('row', 'col'), may hold values 0 or 1
Outputs:
- gradient: float32 [1024, 1024], P('row', 'col')
All inputs are finite; a program needn't handle non-finite values. No bound on the sum of `coeff_mask` or of `intersection_mask` on one device may be relied on, other than what follows from the above.
Results may differ from a plain program's by a relative error of at most 0.0029.
Values may be sent and summed in bfloat16 or wider, within the bound.
A program may use at most 128 MiB of HBM per device.

v0:
```python
import jax
import jax.numpy as jnp
from jax import lax
from jax.sharding import PartitionSpec as P

BLK = 128


def mask_blocks(data, mask):
    rows, cols = data.shape
    shaped = data.reshape(rows // BLK, BLK, cols // BLK, BLK)
    return (shaped * mask.astype(data.dtype)[:, None, :, None]).reshape(rows, cols)


def local(coeffs, intersection, coeff_mask, intersection_mask):
    masked_c = mask_blocks(coeffs, coeff_mask)
    own_rows = lax.all_gather(masked_c, "col", axis=1, tiled=True)
    every_row = lax.all_gather(masked_c, "row", axis=0, tiled=True)
    far_rows = lax.all_to_all(every_row, "col", split_axis=0, concat_axis=1, tiled=True)
    masked_s = mask_blocks(intersection, intersection_mask)
    product = jnp.dot(masked_s, far_rows, preferred_element_type=jnp.float32).astype(jnp.bfloat16)
    partial_sum = lax.dot_general(
        own_rows, product, (((0,), (0,)), ((), ())), preferred_element_type=jnp.float32
    )
    halfway = lax.psum_scatter(partial_sum, "row", scatter_dimension=0, tiled=True)
    gradient = lax.psum_scatter(halfway, "col", scatter_dimension=1, tiled=True)
    return gradient


def solution(mesh):
    return jax.shard_map(
        local,
        mesh=mesh,
        in_specs=(P("row", "col"), P("row", "col"), P("row", "col"), P("row", "col")),
        out_specs=P("row", "col"),
        check_vma=False,
    )
```

profile of v0, /device:TPU:0, one launch (start us, length us, event | category | flops | bytes accessed | tf_op | source)
XLA Modules:
  0.0 457.2 jit_solution(11050008090540716281)
XLA Ops:
  7.4 0.0 all-gather.5.cloned.1.call-start
  7.4 0.7 convert_element_type.9
  8.1 0.1 copy.7
  8.2 0.6 mul.22
  8.8 2.5 bitcast_multiply_fusion.2
  11.2 0.0 all-gather.5.cloned.1.call-update
  11.2 57.2 %all-gather.5.cloned.1.call-done = bf16[16384,256]{1,0:T(8,128)(2,1)} async-done(((bf16[2048,256]{1,0:T(8,128)(2,1)}), bf16[16384,256]{1,0:T(8,128)(2,1)}) %all-gather.5.cloned.1.call-update) | async-done | bytes 8388624 | tf_op jit(solution)/shard_map/all_gather | solution.py:18
  68.5 0.0 copy-start
  68.5 5.8 %all-to-all-start = ((bf16[4,4096,256]{2,1,0:T(8,128)(2,1)}), bf16[4,4096,256]{2,1,0:T(8,128)(2,1)}, u32[]{:S(2)}, u32[]{:S(2)}) async-start(bf16[4,4096,256]{2,1,0:T(8,128)(2,1)} %bitcast.19), calls=%async_computation | async-start | bytes 16777216 | tf_op jit(solution)/shard_map/all_to_all | solution.py:19
  74.3 0.0 all-gather.3.cloned.1.call-start
  74.3 0.5 all-gather.3.cloned.1.call-update
  74.8 0.0 reduce-scatter.3.cloned.1.call-start
  74.9 0.0 copy-done
  74.9 250.5 %all-to-all-done = bf16[4,4096,256]{2,1,0:T(8,128)(2,1)} async-done(((bf16[4,4096,256]{2,1,0:T(8,128)(2,1)}), bf16[4,4096,256]{2,1,0:T(8,128)(2,1)}, u32[]{:S(2)}, u32[]{:S(2)}) %all-to-all-start) | async-done | bytes 8388640 | tf_op jit(solution)/shard_map/all_to_all | solution.py:19
  325.5 12.0 %copy.8 = bf16[4096,4,256]{0,2,1:T(8,128)(2,1)} copy(bf16[4096,4,256]{2,0,1:T(8,128)(2,1)} %bitcast.1) | data formatting | bytes 16777216 | tf_op jit(solution)/shard_map/all_to_all | solution.py:19
  337.4 0.0 all-gather.3.cloned.1.call-done
  337.4 6.2 %mul.25 = bf16[16,128,32,128]{3,2,1,0:T(8,128)(2,1)} broadcast(bf16[16,32]{1,0:T(8,128)(2,1)S(1)} %convert_element_type.10), dimensions={0,2} | broadcast | bytes 16778240 | tf_op jit(solution)/shard_map/mul | solution.py:12
  343.7 34.8 %fusion.2 = f32[1024,1024]{1,0:T(8,128)} fusion(bf16[2048,1024]{1,0:T(8,128)(2,1)} %all-gather.3.cloned.1.call-done, bf16[4096,1024]{0,1:T(8,128)(2,1)} %bitcast.20, bf16[2048,4096]{1,0:T(8,128)(2,1)} %param.5, bf16[256,8,32,128]{3,2,1,0:T(8,128)(2,1)} %bitcast.18), kind=kOutput, calls=%fused_computation.3 | convolution fusion | flops 21485322240 | bytes 50331648 | tf_op jit(solution)/shard_map/dot_general | solution.py:22
  378.5 0.0 reduce-scatter.3.cloned.1.call-update
  378.5 0.0 reduce-scatter.5.cloned.1.call-start
  378.6 49.5 %reduce-scatter.3.cloned.1.call-done = f32[128,1024]{1,0:T(8,128)} async-done(((f32[1024,1024]{1,0:T(8,128)}), f32[128,1024]{1,0:T(8,128)}) %reduce-scatter.3.cloned.1.call-update) | async-done | bytes 524304 | tf_op jit(solution)/shard_map/reduce_scatter | solution.py:25
  428.1 0.0 reduce-scatter.5.cloned.1.call-update
  428.1 21.6 %reduce-scatter.5.cloned.1.call-done = f32[128,256]{1,0:T(8,128)} async-done(((f32[128,1024]{1,0:T(8,128)}), f32[128,256]{1,0:T(8,128)}) %reduce-scatter.5.cloned.1.call-update) | async-done | bytes 131088 | tf_op jit(solution)/shard_map/reduce_scatter | solution.py:26
  (1 shorter events, 0.0 us)
Async XLA Ops:
  7.4 61.1 %all-gather.5.cloned.1.call-start = ((), (), s32[]{:S(2)}) async-start(), calls=%async_computation.4 | async-start | bytes 9437184 | tf_op jit(solution)/shard_map/all_gather | solution.py:18
  68.5 6.4 %copy-start = (s32[16,32]{1,0:T(8,128)S(1)}, s32[16,32]{1,0:T(8,128)}, u32[]{:S(2)}) copy-start(s32[16,32]{1,0:T(8,128)} %param.7) | copy-start | bytes 6148
  68.5 257.0 %all-to-all-start = ((bf16[4,4096,256]{2,1,0:T(8,128)(2,1)}), bf16[4,4096,256]{2,1,0:T(8,128)(2,1)}, u32[]{:S(2)}, u32[]{:S(2)}) async-start(bf16[4,4096,256]{2,1,0:T(8,128)(2,1)} %bitcast.19), calls=%async_computation | async-start | bytes 16777216 | tf_op jit(solution)/shard_map/all_to_all | solution.py:19
  74.3 263.2 %all-gather.3.cloned.1.call-start = ((), (), s32[]{:S(2)}) async-start(), calls=%async_computation.3 | async-start | bytes 5242880 | tf_op jit(solution)/shard_map/all_gather | solution.py:17
  74.8 353.3 %reduce-scatter.3.cloned.1.call-start = ((), (), s32[]{:S(2)}) async-start(), calls=%async_computation.5 | async-start | bytes 4718592 | tf_op jit(solution)/shard_map/reduce_scatter | solution.py:25
  378.5 71.2 %reduce-scatter.5.cloned.1.call-start = ((), (), s32[]{:S(2)}) async-start(), calls=%async_computation.6 | async-start | bytes 655360 | tf_op jit(solution)/shard_map/reduce_scatter | solution.py:26
Sparse Core Ops, SparseCore 0:
  11.4 57.0 all-gather.4
  378.6 49.4 reduce-scatter.2
Sparse Core Ops, SparseCore 1:
  76.3 161.2 all-gather.2
  428.2 21.5 reduce-scatter.4
where the time goes:
time: 458 us; the launch traced here: 457 us
  waiting for transfers between devices  380 us (83%)
  matrix products  34.8 us (8%)
  local copies, waits for them, and re-layouts  18.9 us (4%)
  between operations  14.9 us (3%)
  starting transfers between devices  5.9 us (1%)
    all_to_all x1, waiting for transfers between devices, local(): lax.all_to_all(every_row, 'col', split_axis=0, concat_axis=1, tiled=True)  251 us
    all_gather x1, waiting for transfers between devices, local(): every_row = lax.all_gather(masked_c, 'row', axis=0, tiled=True)  57.2 us
    reduce_scatter x1, waiting for transfers between devices, local(): lax.psum_scatter(partial_sum, 'row', scatter_dimension=0, tiled=True)  49.5 us
    dot_general x1, matrix products, local(): lax.dot_general(own_rows, product, (((0,), (0,)), ((), ())), preferred_el...  34.8 us
    reduce_scatter x1, waiting for transfers between devices, local(): gradient = lax.psum_scatter(halfway, 'col', scatter_dimension=1, tiled=True)  21.6 us
    all_to_all x1, local copies, waits for them, and re-layouts, local(): lax.all_to_all(every_row, 'col', split_axis=0, concat_axis=1, tiled=True)  12 us
  transfers between devices with their start and end apart: 5, of which 4 were waited for; matrix products, arithmetic and copies ran while one was open for 3% of the time, Pallas kernels for 0%

commit v1 on v0

v1 whole, which is shorter than its diff:
```python
import functools

import jax
import jax.numpy as jnp
from jax import lax
from jax.experimental import pallas as pl
from jax.experimental.pallas import tpu as pltpu
from jax.sharding import PartitionSpec as P

BLK = 128
CHUNKS = 4
BF = jnp.bfloat16
F32 = jnp.float32


def kernel(
    rn, zn, cmask, smask, c_ref, s_hbm, out_ref,
    s_buf, rows, rows_t, cols, prod, g_own, g_sib, g_got, x_out, x_in, z_out, z_in,
    s_sem, up_send, dn_send, z_recv, ring_send, ring_recv, sib_send, sib_recv, loc_sem,
    gs_send, gs_recv, xs_send, xs_recv, zs_send, zs_recv,
):
    n = rn // 2
    half = n // 2
    row, z = lax.axis_index("row"), lax.axis_index("col")
    chip, core = row // 2, row % 2
    height, w = c_ref.shape
    ch = height // CHUNKS
    hb = out_ref.shape[0]

    def pos_of(p):
        return jnp.where(p % 2 == 0, p // 2, n - 1 - p // 2)

    def chip_at(pos):
        return jnp.where(pos < half, 2 * pos, 2 * (n - 1 - pos) + 1)

    def dev(p, k, zz):
        return (2 * p + k, zz)

    pos = pos_of(chip)
    step = 1 - 2 * core
    dist = ((pos - pos_of(z)) * step + n) % n
    holder = dist == 0
    ahead = dev(chip_at((pos + step + n) % n), core, z)
    sibling = dev(chip, 1 - core, z)

    def remote(src, dst, ss, rs, target):
        return pltpu.make_async_remote_copy(
            src_ref=src, dst_ref=dst, send_sem=ss, recv_sem=rs,
            device_id=target, device_id_type=pl.DeviceIdType.MESH,
        )

    def part(q):
        return pl.ds(pl.multiple_of(q * ch, ch), ch)

    def s_copy(q):
        return pltpu.make_async_copy(s_hbm.at[part(q)], s_buf.at[part(q)], s_sem.at[q])

    def up_copy(s, q):
        ref = rows.at[s, part(q)]
        return remote(ref, ref, up_send.at[s, q], z_recv.at[s, q], (row, jnp.minimum(z + 1, zn - 1)))

    def dn_copy(s, q):
        ref = rows.at[s, part(q)]
        return remote(ref, ref, dn_send.at[s, q], z_recv.at[s, q], (row, jnp.maximum(z - 1, 0)))

    def ring_copy(s, q, src):
        return remote(src.at[part(q)], cols.at[s, core, part(q)], ring_send.at[s, q], ring_recv.at[s, q], ahead)

    def sib_copy(s, q, src):
        return remote(src.at[part(q)], cols.at[s, core, part(q)], sib_send.at[s, q], sib_recv.at[s, q], sibling)

    def loc_copy(s, q):
        return pltpu.make_async_copy(rows.at[s, part(q)], cols.at[s, core, part(q)], loc_sem.at[s, q])

    for q in range(CHUNKS):
        s_copy(q).start()

    barrier = pltpu.get_barrier_semaphore()
    for d in range(1, n):
        pl.semaphore_signal(barrier, inc=1, device_id=dev((chip + d) % n, core, z), device_id_type=pl.DeviceIdType.MESH)
    for d in range(1, zn):
        pl.semaphore_signal(barrier, inc=1, device_id=(row, (z + d) % zn), device_id_type=pl.DeviceIdType.MESH)
    pl.semaphore_signal(barrier, inc=1, device_id=sibling, device_id_type=pl.DeviceIdType.MESH)

    def mask_c(i, carry):
        at = pl.ds(pl.multiple_of(i * BLK, BLK), BLK)
        for j in range(w // BLK):
            m = jnp.full((BLK, BLK), cmask[i, j].astype(F32), F32).astype(BF)
            rows[z, at, j * BLK:(j + 1) * BLK] = c_ref[at, j * BLK:(j + 1) * BLK] * m
        return carry

    lax.fori_loop(0, height // BLK, mask_c, 0)
    pl.semaphore_wait(barrier, n - 1 + zn - 1 + 1)

    def mask_s(i, carry):
        at = pl.ds(pl.multiple_of(i * BLK, BLK), BLK)
        for j in range(s_buf.shape[1] // BLK):
            m = jnp.full((BLK, BLK), smask[i, j].astype(F32), F32).astype(BF)
            s_buf[at, j * BLK:(j + 1) * BLK] = s_buf[at, j * BLK:(j + 1) * BLK] * m
        return carry

    def arrive(s, q, t, side):
        ok = jnp.logical_and(s >= 0, s < zn)
        if side:
            ok = jnp.logical_and(ok, t > 0)

        @pl.when(ok)
        def _():
            @pl.when(t > 0)
            def _():
                up_copy(s, q).wait_recv()

            if side == 0:
                @pl.when(z < zn - 1)
                def _():
                    up_copy(s, q).start()

            @pl.when(jnp.logical_and(z > 0, (t == 0) if side == 0 else True))
            def _():
                dn_copy(s, q).start()

            @pl.when(holder)
            def _():
                ring_copy(s, q, rows.at[s]).start()
                sib_copy(s, q, rows.at[s]).start()
                loc_copy(s, q).start()

    def relay(s, q, t, side):
        ok = jnp.logical_and(s >= 0, s < zn)
        if side:
            ok = jnp.logical_and(ok, t > 0)

        @pl.when(ok)
        def _():
            rows_t[s, :, part(q)] = rows[s, part(q)].T

            @pl.when(jnp.logical_not(holder))
            def _():
                src = cols.at[s, core]
                ring_copy(s, q, src).wait_recv()

                @pl.when(dist < n - 1)
                def _():
                    ring_copy(s, q, src).start()

                sib_copy(s, q, src).start()

    def multiply(s, q, t, side):
        ok = jnp.logical_and(s >= 0, s < zn)
        ok = jnp.logical_and(ok, t > (1 if side else 0))

        @pl.when(ok)
        def _():
            @pl.when(q == 0)
            def _():
                def settle(qq, carry):
                    @pl.when(holder)
                    def _():
                        loc_copy(s, qq).wait()

                    sib_copy(s, qq, cols.at[s, core]).wait_recv()
                    return carry

                lax.fori_loop(0, CHUNKS, settle, 0)

            total = jnp.dot(s_buf[part(q), :height], cols[s, 0], preferred_element_type=F32)
            total += jnp.dot(s_buf[part(q), height:], cols[s, 1], preferred_element_type=F32)
            prod[s, part(q)] = total.astype(BF)

    def tick(i, carry):
        t, q = i // CHUNKS, i % CHUNKS

        @pl.when(t < zn)
        def _():
            arrive(z - t, q, t, 0)
            arrive(z + t, q, t, 1)

        @pl.when(t == 0)
        def _():
            s_copy(q).wait()
            lax.fori_loop(q * (ch // BLK), (q + 1) * (ch // BLK), mask_s, 0)

        @pl.when(t < zn)
        def _():
            relay(z - t, q, t, 0)
            relay(z + t, q, t, 1)

        multiply(z - t + 1, q, t, 0)
        multiply(z + t - 1, q, t, 1)
        return carry

    lax.fori_loop(0, (zn + 1) * CHUNKS, tick, 0)

    def gs_copy(c):
        return remote(g_sib.at[c], g_got.at[c], gs_send.at[c], gs_recv.at[c], sibling)

    def contract(i, carry):
        c = (z + 1 + i) % zn

        def rowblock(s, carry):
            got = jnp.dot(rows_t[s], prod[c], preferred_element_type=F32)
            per = w // hb
            for b in range(per // 2):
                lo = got[2 * b * hb:(2 * b + 1) * hb]
                hi = got[(2 * b + 1) * hb:(2 * b + 2) * hb]
                g_own[c, s * (per // 2) + b] = jnp.where(core == 0, lo, hi)
                g_sib[c, s * (per // 2) + b] = jnp.where(core == 0, hi, lo)
            return carry

        lax.fori_loop(0, zn, rowblock, 0)
        gs_copy(c).start()
        return carry

    lax.fori_loop(0, zn, contract, 0)

    def xs_copy(c, d):
        target = (chip + d) % n
        return remote(x_out.at[c, target], x_in.at[c, d], xs_send.at[c, d], xs_recv.at[c, d], dev(target, core, z))

    def spread(i, carry):
        c = (z + 1 + i) % zn
        gs_copy(c).wait_recv()
        total = g_own[c] + g_got[c]
        g_own[c] = total
        x_out[c] = total.astype(BF)
        for d in range(1, n):
            xs_copy(c, d).start()
        return carry

    lax.fori_loop(0, zn, spread, 0)

    def zs_copy(d):
        return remote(z_out.at[d], z_in.at[d], zs_send.at[d], zs_recv.at[d], (row, (z + d) % zn))

    def plane_sum(c):
        total = g_own[c, chip]
        for d in range(1, n):
            xs_copy(c, d).wait_recv()
            total += x_in[c, d].astype(F32)
        return total

    def onward(d, carry):
        c = (z + d) % zn
        z_out[d] = plane_sum(c).astype(BF)
        zs_copy(d).start()
        return carry

    lax.fori_loop(1, zn, onward, 0)
    total = plane_sum(z)
    for d in range(1, zn):
        zs_copy(d).wait_recv()
        total += z_in[d].astype(F32)
    out_ref[...] = total

    def drain(i, carry):
        s, q = i // CHUNKS, i % CHUNKS

        @pl.when(jnp.logical_and(s <= z, z < zn - 1))
        def _():
            up_copy(s, q).wait_send()

        @pl.when(jnp.logical_and(s >= z, z > 0))
        def _():
            dn_copy(s, q).wait_send()

        @pl.when(dist < n - 1)
        def _():
            ring_copy(s, q, cols.at[s, core]).wait_send()

        sib_copy(s, q, cols.at[s, core]).wait_send()
        return carry

    lax.fori_loop(0, zn * CHUNKS, drain, 0)

    def drain_sums(c, carry):
        gs_copy(c).wait_send()
        for d in range(1, n):
            xs_copy(c, d).wait_send()
        return carry

    lax.fori_loop(0, zn, drain_sums, 0)
    for d in range(1, zn):
        zs_copy(d).wait_send()


def local(rn, zn, coeffs, intersection, coeff_mask, intersection_mask):
    height, w = coeffs.shape
    width = intersection.shape[1]
    n = rn // 2
    hb = zn * w // rn
    dma = pltpu.SemaphoreType.DMA
    flops = 2 * height * width * w * zn + 2 * height * (w * zn) ** 2
    return pl.pallas_call(
        functools.partial(kernel, rn, zn),
        out_shape=jax.ShapeDtypeStruct((hb, w), F32),
        in_specs=[
            pl.BlockSpec(memory_space=pltpu.SMEM),
            pl.BlockSpec(memory_space=pltpu.SMEM),
            pl.BlockSpec(memory_space=pltpu.VMEM),
            pl.BlockSpec(memory_space=pl.ANY),
        ],
        out_specs=pl.BlockSpec(memory_space=pltpu.VMEM),
        scratch_shapes=[
            pltpu.VMEM((height, width), BF),
            pltpu.VMEM((zn, height, w), BF),
            pltpu.VMEM((zn, w, height), BF),
            pltpu.VMEM((zn, 2, height, w), BF),
            pltpu.VMEM((zn, height, w), BF),
            pltpu.VMEM((zn, n, hb, w), F32),
            pltpu.VMEM((zn, n, hb, w), F32),
            pltpu.VMEM((zn, n, hb, w), F32),
            pltpu.VMEM((zn, n, hb, w), BF),
            pltpu.VMEM((zn, n, hb, w), BF),
            pltpu.VMEM((zn, hb, w), BF),
            pltpu.VMEM((zn, hb, w), BF),
            dma((CHUNKS,)),
        ] + [dma((zn, CHUNKS))] * 8 + [
            dma((zn,)), dma((zn,)),
            dma((zn, n)), dma((zn, n)),
            dma((zn,)), dma((zn,)),
        ],
        compiler_params=pltpu.CompilerParams(
            collective_id=0, has_side_effects=True, vmem_limit_bytes=60 * 1024 * 1024
        ),
        cost_estimate=pl.CostEstimate(flops=flops, bytes_accessed=2 * height * width, transcendentals=0),
    )(coeff_mask, intersection_mask, coeffs, intersection)


def solution(mesh):
    return jax.shard_map(
        functools.partial(local, mesh.shape["row"], mesh.shape["col"]),
        mesh=mesh,
        in_specs=(P("row", "col"), P("row", "col"), P("row", "col"), P("row", "col")),
        out_specs=P("row", "col"),
        check_vma=False,
    )
```

time: 458 us -> 125 us (0.27)
  waiting for transfers between devices: 380 us -> 0 us
  Pallas kernels: 0 us -> 122 us
  matrix products: 34.8 us -> 0 us
  local copies, waits for them, and re-layouts: 18.9 us -> 2.92 us
  between operations: 14.9 us -> 0.01 us
  starting transfers between devices: 5.9 us -> 0 us
    all_to_all x1 -> x0, waiting for transfers between devices: 251 us -> none  [local(): lax.all_to_all(every_row, 'col', split_axis=0, concat_axis=1, tiled=True)]
    pallas_call x0 -> x1, Pallas kernels: none -> 122 us  [local(): pl.pallas_call(functools.partial(kernel, rn, zn), out_shape=jax.ShapeDtyp...]
    reduce_scatter x2 -> x0, waiting for transfers between devices: 71.2 us -> none  [the longest x1 49.5 us: local(): lax.psum_scatter(partial_sum, 'row', scatter_dimension=0, tiled=True)]
    all_gather x2 -> x0, waiting for transfers between devices: 57.2 us -> none  [the longest x1 57.2 us: local(): every_row = lax.all_gather(masked_c, 'row', axis=0, tiled=True)]
    dot_general x1 -> x0, matrix products: 34.8 us -> none  [local(): lax.dot_general(own_rows, product, (((0,), (0,)), ((), ())), preferred_el...]
    all_to_all x1 -> x0, local copies, waits for them, and re-layouts: 12 us -> none  [local(): lax.all_to_all(every_row, 'col', split_axis=0, concat_axis=1, tiled=True)]
    mul x2 -> x0, local copies, waits for them, and re-layouts: 6.85 us -> none  [mask_blocks(): shaped * mask.astype(data.dtype)[:, None, :, None]]
    all_to_all x1 -> x0, starting transfers between devices: 5.77 us -> none  [local(): lax.all_to_all(every_row, 'col', split_axis=0, concat_axis=1, tiled=True)]
  transfers between devices with their start and end apart: 5 -> 0, of which waited for: 4 -> 0; matrix products, arithmetic and copies ran while one was open for 3% -> 0% of each run, Pallas kernels for 0% -> 0%
where the time goes in v1:
time: 125 us
  Pallas kernels  122 us (98%)
  local copies, waits for them, and re-layouts  2.92 us (2%)
    pallas_call x1, Pallas kernels, local(): pl.pallas_call(functools.partial(kernel, rn, zn), out_shape=jax.ShapeDtyp...  122 us
    unnamed x2, local copies, waits for them, and re-layouts  2.92 us

profile of v1, /device:TPU:0, one launch (start us, length us, event | category | flops | bytes accessed | tf_op | source)
XLA Modules:
  0.0 124.7 jit_solution(9027299806630322643)
XLA Ops:
  0.0 1.4 %copy.5.cmask = s32[16,2]{1,0:T(8,128)} copy(s32[16,2]{0,1:T(2,128)} %param.6) | data formatting | bytes 256 | tf_op args[2]
  1.4 121.8 %shard_map.46 = f32[128,256]{1,0:T(8,128)} custom-call(s32[16,2]{1,0:T(8,128)} %copy.5.cmask, s32[16,32]{1,0:T(8,128)} %smask.1, bf16[2048,256]{1,0:T(8,128)(2,1)} %c_ref.1, bf16[2048,4096]{1,0:T(8,128)(2,1)} %s_hbm.1), custom_call_target="tpu_custom_call" | custom-call | flops 21474836480 | bytes 16777216 | tf_op jit(solution)/shard_map/pallas_call | solution.py:293
  123.1 1.6 %copy.7 = f32[128,256]{1,0:T(8,128)} copy(f32[128,256]{1,0:T(8,128)} %shard_map.46) | data formatting | bytes 262144

commit v2 on v1

--- a/solution.py
+++ b/solution.py
@@ -8,7 +8,8 @@
 from jax.sharding import PartitionSpec as P
 
 BLK = 128
-CHUNKS = 4
+CHUNKS = 8
+PAIRS = CHUNKS // 2
 BF = jnp.bfloat16
 F32 = jnp.float32
 
@@ -37,10 +38,17 @@
         return (2 * p + k, zz)
 
     pos = pos_of(chip)
-    step = 1 - 2 * core
-    dist = ((pos - pos_of(z)) * step + n) % n
-    holder = dist == 0
-    ahead = dev(chip_at((pos + step + n) % n), core, z)
+    holder = chip == z
+
+    def way(q):
+        return 1 - 2 * (core)
+
+    def dist(q):
+        return ((pos - pos_of(z)) * way(q) + n) % n
+
+    def ahead(q):
+        return dev(chip_at((pos + way(q) + n) % n), core, z)
+
     sibling = dev(chip, 1 - core, z)
 
     def remote(src, dst, ss, rs, target):
@@ -64,7 +72,7 @@
         return remote(ref, ref, dn_send.at[s, q], z_recv.at[s, q], (row, jnp.maximum(z - 1, 0)))
 
     def ring_copy(s, q, src):
-        return remote(src.at[part(q)], cols.at[s, core, part(q)], ring_send.at[s, q], ring_recv.at[s, q], ahead)
+        return remote(src.at[part(q)], cols.at[s, core, part(q)], ring_send.at[s, q], ring_recv.at[s, q], ahead(q))
 
     def sib_copy(s, q, src):
         return remote(src.at[part(q)], cols.at[s, core, part(q)], sib_send.at[s, q], sib_recv.at[s, q], sibling)
@@ -139,7 +147,7 @@
                 src = cols.at[s, core]
                 ring_copy(s, q, src).wait_recv()
 
-                @pl.when(dist < n - 1)
+                @pl.when(dist(q) < n - 1)
                 def _():
                     ring_copy(s, q, src).start()
 
@@ -163,38 +171,52 @@
 
                 lax.fori_loop(0, CHUNKS, settle, 0)
 
-            total = jnp.dot(s_buf[part(q), :height], cols[s, 0], preferred_element_type=F32)
-            total += jnp.dot(s_buf[part(q), height:], cols[s, 1], preferred_element_type=F32)
-            prod[s, part(q)] = total.astype(BF)
+            at = pl.ds(pl.multiple_of(q * 2 * ch, 2 * ch), 2 * ch)
+            total = jnp.dot(s_buf[at, :height], cols[s, 0], preferred_element_type=F32)
+            total += jnp.dot(s_buf[at, height:], cols[s, 1], preferred_element_type=F32)
+            prod[s, at] = total.astype(BF)
 
     def tick(i, carry):
-        t, q = i // CHUNKS, i % CHUNKS
+        t = i // PAIRS
+        first = 2 * (i % PAIRS)
 
         @pl.when(t < zn)
         def _():
-            arrive(z - t, q, t, 0)
-            arrive(z + t, q, t, 1)
+            for q in (first, first + 1):
+                arrive(z - t, q, t, 0)
+                arrive(z + t, q, t, 1)
 
         @pl.when(t == 0)
         def _():
-            s_copy(q).wait()
-            lax.fori_loop(q * (ch // BLK), (q + 1) * (ch // BLK), mask_s, 0)
-
-        @pl.when(t < zn)
-        def _():
-            relay(z - t, q, t, 0)
-            relay(z + t, q, t, 1)
-
-        multiply(z - t + 1, q, t, 0)
-        multiply(z + t - 1, q, t, 1)
-        return carry
-
-    lax.fori_loop(0, (zn + 1) * CHUNKS, tick, 0)
+            for q in (first, first + 1):
+                s_copy(q).wait()
+            lax.fori_loop(first * (ch // BLK), (first + 2) * (ch // BLK), mask_s, 0)
+
+        for parity in range(2):
+            late = i - dist(parity)
+
+            @pl.when(jnp.logical_and(late >= 0, late < zn * PAIRS))
+            def _():
+                t, q = late // PAIRS, 2 * (late % PAIRS) + parity
+                relay(z - t, q, t, 0)
+                relay(z + t, q, t, 1)
+
+        late = i - (n - 1)
+
+        @pl.when(late >= PAIRS)
+        def _():
+            t, q = late // PAIRS, late % PAIRS
+            multiply(z - t + 1, q, t, 0)
+            multiply(z + t - 1, q, t, 1)
+
+        return carry
+
+    lax.fori_loop(0, (zn + 1) * PAIRS + n - 1, tick, 0)
 
     def gs_copy(c):
         return remote(g_sib.at[c], g_got.at[c], gs_send.at[c], gs_recv.at[c], sibling)
 
-    def contract(i, carry):
+    def contract(i):
         c = (z + 1 + i) % zn
 
         def rowblock(s, carry):
@@ -209,15 +231,12 @@
 
         lax.fori_loop(0, zn, rowblock, 0)
         gs_copy(c).start()
-        return carry
-
-    lax.fori_loop(0, zn, contract, 0)
 
     def xs_copy(c, d):
         target = (chip + d) % n
         return remote(x_out.at[c, target], x_in.at[c, d], xs_send.at[c, d], xs_recv.at[c, d], dev(target, core, z))
 
-    def spread(i, carry):
+    def spread(i):
         c = (z + 1 + i) % zn
         gs_copy(c).wait_recv()
         total = g_own[c] + g_got[c]
@@ -225,9 +244,19 @@
         x_out[c] = total.astype(BF)
         for d in range(1, n):
             xs_copy(c, d).start()
-        return carry
-
-    lax.fori_loop(0, zn, spread, 0)
+
+    def stage(i, carry):
+        @pl.when(i < zn)
+        def _():
+            contract(i)
+
+        @pl.when(i > 0)
+        def _():
+            spread(i - 1)
+
+        return carry
+
+    lax.fori_loop(0, zn + 1, stage, 0)
 
     def zs_copy(d):
         return remote(z_out.at[d], z_in.at[d], zs_send.at[d], zs_recv.at[d], (row, (z + d) % zn))
@@ -263,7 +292,7 @@
         def _():
             dn_copy(s, q).wait_send()
 
-        @pl.when(dist < n - 1)
+        @pl.when(dist(q) < n - 1)
         def _():
             ring_copy(s, q, cols.at[s, core]).wait_send()
 

time: 125 us -> 118 us (0.944)
  Pallas kernels: 122 us -> 115 us
    pallas_call x1, Pallas kernels: 122 us -> 115 us  [local(): pl.pallas_call(functools.partial(kernel, rn, zn), out_shape=jax.ShapeDtyp...]
where the time goes in v2:
time: 118 us
  Pallas kernels  115 us (97%)
  local copies, waits for them, and re-layouts  2.92 us (2%)
    pallas_call x1, Pallas kernels, local(): pl.pallas_call(functools.partial(kernel, rn, zn), out_shape=jax.ShapeDtyp...  115 us
    unnamed x2, local copies, waits for them, and re-layouts  2.92 us

profile of v2, /device:TPU:0, one launch (start us, length us, event | category | flops | bytes accessed | tf_op | source)
XLA Modules:
  0.0 118.0 jit_solution(17803836096499092858)
XLA Ops:
  0.0 1.4 %copy.5.cmask = s32[16,2]{1,0:T(8,128)} copy(s32[16,2]{0,1:T(2,128)} %param.6) | data formatting | bytes 256 | tf_op args[2]
  1.4 115.1 %shard_map.46 = f32[128,256]{1,0:T(8,128)} custom-call(s32[16,2]{1,0:T(8,128)} %copy.5.cmask, s32[16,32]{1,0:T(8,128)} %smask.1, bf16[2048,256]{1,0:T(8,128)(2,1)} %c_ref.1, bf16[2048,4096]{1,0:T(8,128)(2,1)} %s_hbm.1), custom_call_target="tpu_custom_call" | custom-call | flops 21474836480 | bytes 16777216 | tf_op jit(solution)/shard_map/pallas_call | solution.py:322
  116.5 1.6 %copy.7 = f32[128,256]{1,0:T(8,128)} copy(f32[128,256]{1,0:T(8,128)} %shard_map.46) | data formatting | bytes 262144

commit v3 on v2

--- a/solution.py
+++ b/solution.py
@@ -140,8 +140,6 @@
 
         @pl.when(ok)
         def _():
-            rows_t[s, :, part(q)] = rows[s, part(q)].T
-
             @pl.when(jnp.logical_not(holder))
             def _():
                 src = cols.at[s, core]
@@ -152,6 +150,8 @@
                     ring_copy(s, q, src).start()
 
                 sib_copy(s, q, src).start()
+
+            rows_t[s, :, part(q)] = rows[s, part(q)].T
 
     def multiply(s, q, t, side):
         ok = jnp.logical_and(s >= 0, s < zn)

time: 118 us -> 118 us (level)
  no operation moved by 1% of the time
where the time goes in v3:
time: 118 us
  Pallas kernels  115 us (97%)
  local copies, waits for them, and re-layouts  2.92 us (2%)
    pallas_call x1, Pallas kernels, local(): pl.pallas_call(functools.partial(kernel, rn, zn), out_shape=jax.ShapeDtyp...  115 us
    unnamed x2, local copies, waits for them, and re-layouts  2.92 us

profile of v3, /device:TPU:0, one launch (start us, length us, event | category | flops | bytes accessed | tf_op | source)
XLA Modules:
  0.0 118.1 jit_solution(6869798751517734220)
XLA Ops:
  0.0 1.4 %copy.5.cmask = s32[16,2]{1,0:T(8,128)} copy(s32[16,2]{0,1:T(2,128)} %param.6) | data formatting | bytes 256 | tf_op args[2]
  1.4 115.2 %shard_map.46 = f32[128,256]{1,0:T(8,128)} custom-call(s32[16,2]{1,0:T(8,128)} %copy.5.cmask, s32[16,32]{1,0:T(8,128)} %smask.1, bf16[2048,256]{1,0:T(8,128)(2,1)} %c_ref.1, bf16[2048,4096]{1,0:T(8,128)(2,1)} %s_hbm.1), custom_call_target="tpu_custom_call" | custom-call | flops 21474836480 | bytes 16777216 | tf_op jit(solution)/shard_map/pallas_call | solution.py:322
  116.5 1.6 %copy.7 = f32[128,256]{1,0:T(8,128)} copy(f32[128,256]{1,0:T(8,128)} %shard_map.46) | data formatting | bytes 262144
